TPU v7x, 32 devices: a whole 2x2x4 slice. The times are simulated.
32 devices in a mesh: head: 2 (over y), blk: 16 (over z, x, core).
Axes of the slice: x: 2, y: 2, z: 4, core: 2. Of those that a mesh axis runs over, the one named last changes fastest.
Arguments:
- queries: bfloat16 [4096, 6144], P(('blk', 'head')), may hold values from -4.5 to 4.5
- key_states: bfloat16 [4096, 6144], P(('blk', 'head')), may hold values from -4.5 to 4.5
- value_states: bfloat16 [4096, 6144], P(('blk', 'head')), may hold values from -6 to 6
- block_lists: int32 [32, 8], P('blk'), may hold values from 0 to 31, as said below
- block_counts: int32 [32], P('blk'), may hold values from 1 to 8
- tile_order: int32 [32], replicated, may hold values from 0 to 31, each once
Outputs:
- attended: bfloat16 [4096, 6144], P(('blk', 'head'))
Inputs may be any that keep to these rules, and one draw needn't show every extreme that they name: `block_lists`: entry 0 of row t is t itself; the entries of a row are distinct, and each names a tile whose shard of 2 tiles lies at most 3 shards from the shard of t, counted cyclically over the clip.
All inputs are finite; a program needn't handle non-finite values.
Results may differ from a plain program's by a relative error of at most 0.0095.
Values may be sent and summed in bfloat16 or wider, within the bound.
A program may use at most 128 MiB of HBM per device.

v0:
```python
import jax
import jax.numpy as jnp
from jax import lax
from jax.sharding import PartitionSpec as P

H = 48
DH = 128
TILE = 128
REACH = 3
SLOTS = 8


def shifted(block, axis, distance):
    devices = range(lax.axis_size(axis))
    route = [((i - distance) % len(devices), i) for i in devices]
    return lax.ppermute(block, axis, route)


def body(queries, key_states, value_states, block_lists, block_counts, tile_order):
    cycle_size = lax.axis_size("blk")
    group_size = lax.axis_size("head")
    heads_local = H // group_size
    q_heads, k_heads, v_heads = (
        lax.all_to_all(queries, "head", split_axis=1, concat_axis=0, tiled=True),
        lax.all_to_all(key_states, "head", split_axis=1, concat_axis=0, tiled=True),
        lax.all_to_all(value_states, "head", split_axis=1, concat_axis=0, tiled=True),
    )
    shard_tok = q_heads.shape[0]
    tile_count = shard_tok // TILE
    tile_shape = (tile_count, TILE, heads_local, DH)
    q_tiles = q_heads.reshape(tile_shape)
    local_pair = jnp.stack((k_heads.reshape(tile_shape), v_heads.reshape(tile_shape)))
    pieces = {0: local_pair}
    current = shifted(local_pair, "blk", -REACH)
    pieces[REACH] = current
    for hop_index in range(2 * REACH):
        current = shifted(current, "blk", 1)
        offset = REACH - 1 - hop_index
        if offset != 0:
            pieces[offset] = current
    window = jnp.concatenate([pieces[offset] for offset in range(-REACH, REACH + 1)], axis=1)
    blk_index = lax.axis_index("blk")
    shard_of = block_lists // tile_count
    slot_window = (
        shard_of - blk_index + REACH
    ) % cycle_size * tile_count + block_lists % tile_count
    query_tile = blk_index * tile_count + jnp.arange(tile_count, dtype=jnp.int32)
    distance = (
        jnp.abs(tile_order[query_tile][:, None] - tile_order[block_lists]).astype(jnp.float32)
        / tile_order.shape[0]
    )
    valid = jnp.arange(SLOTS, dtype=jnp.int32)[None, :] < block_counts[:, None]
    head_index = lax.axis_index("head") * heads_local + jnp.arange(heads_local, dtype=jnp.int32)
    slopes = 8.0 * jnp.power(2.0, -8.0 * head_index.astype(jnp.float32) / H)
    scale = DH ** (-0.5)

    def one_tile(items):
        q_tile, where_index, dist_row, valid_row = items
        chosen = window[:, where_index]
        scores = (
            jnp.einsum("ihd,cjhd->hicj", q_tile, chosen[0], preferred_element_type=jnp.float32)
            * scale
        )
        scores = scores - slopes[:, None, None, None] * dist_row[None, None, :, None]
        scores = jnp.where(valid_row[None, None, :, None], scores, -1e30).reshape(
            heads_local, TILE, SLOTS * TILE
        )
        top = jnp.max(scores, axis=-1)
        weights = jnp.exp(scores - top[..., None]).astype(jnp.bfloat16)
        total = jnp.sum(weights.astype(jnp.float32), axis=-1)
        mixed = jnp.einsum(
            "hik,khd->ihd",
            weights,
            chosen[1].reshape(SLOTS * TILE, heads_local, DH),
            preferred_element_type=jnp.float32,
        )
        return (mixed / total.T[:, :, None]).astype(jnp.bfloat16)

    out_tiles = lax.map(one_tile, (q_tiles, slot_window, distance, valid))
    return lax.all_to_all(
        out_tiles.reshape(shard_tok, heads_local * DH),
        "head",
        split_axis=0,
        concat_axis=1,
        tiled=True,
    )


def solution(mesh):
    in_specs = (
        P(("blk", "head"), None),
        P(("blk", "head"), None),
        P(("blk", "head"), None),
        P("blk", None),
        P("blk"),
        P(),
    )
    out_specs = P(("blk", "head"), None)
    return jax.shard_map(body, mesh=mesh, in_specs=in_specs, out_specs=out_specs, check_vma=False)
```

profile of v0, /device:TPU:0, one launch (start us, length us, event | category | flops | bytes accessed | tf_op | source)
XLA Modules:
  0.0 528.6 jit_solution(16725005537391740156)
XLA Ops:
  8.3 18.9 %all-to-all-done = bf16[128,2,3072]{2,0,1:T(8,128)(2,1)S(1)} async-done(((bf16[128,2,3072]{2,0,1:T(8,128)(2,1)}), bf16[128,2,3072]{2,0,1:T(8,128)(2,1)S(1)}, u32[]{:S(2)}, u32[]{:S(2)}) %all-to-all-start) | async-done | bytes 1572896 | tf_op jit(solution)/shard_map/all_to_all | solution.py:25
  27.2 4.6 all-to-all-start.1
  32.2 18.7 %all-to-all-done.1 = bf16[128,2,3072]{2,0,1:T(8,128)(2,1)} async-done(((bf16[128,2,3072]{2,0,1:T(8,128)(2,1)}), bf16[128,2,3072]{2,0,1:T(8,128)(2,1)}, u32[]{:S(2)}, u32[]{:S(2)}) %all-to-all-start.1) | async-done | bytes 1572896 | tf_op jit(solution)/shard_map/all_to_all | solution.py:26
  55.3 65.7 %collective-permute-done = bf16[2,2,128,24,128]{4,3,2,1,0:T(8,128)(2,1)S(1)} collective-permute-done((bf16[2,2,128,24,128]{4,3,2,1,0:T(8,128)(2,1)S(1)}, bf16[2,2,128,24,128]{4,3,2,1,0:T(8,128)(2,1)S(1)}, u32[]{:S(2)}, u32[]{:S(2)}) %collective-permute-start) | collective-permute-done | bytes 3145760 | tf_op jit(solution)/shard_map/ppermute | solution.py:16
  125.6 36.5 %collective-permute-done.1 = bf16[2,2,128,24,128]{4,3,2,1,0:T(8,128)(2,1)S(1)} collective-permute-done((bf16[2,2,128,24,128]{4,3,2,1,0:T(8,128)(2,1)S(1)}, bf16[2,2,128,24,128]{4,3,2,1,0:T(8,128)(2,1)S(1)}, u32[]{:S(2)}, u32[]{:S(2)}) %collective-permute-start.1) | collective-permute-done | bytes 3145760 | tf_op jit(solution)/shard_map/ppermute | solution.py:16
  163.8 39.4 %collective-permute-done.2 = bf16[2,2,128,24,128]{4,3,2,1,0:T(8,128)(2,1)S(1)} collective-permute-done((bf16[2,2,128,24,128]{4,3,2,1,0:T(8,128)(2,1)S(1)}, bf16[2,2,128,24,128]{4,3,2,1,0:T(8,128)(2,1)S(1)}, u32[]{:S(2)}, u32[]{:S(2)}) %collective-permute-start.2) | collective-permute-done | bytes 3145760 | tf_op jit(solution)/shard_map/ppermute | solution.py:16
  204.9 39.4 %collective-permute-done.3 = bf16[2,2,128,24,128]{4,3,2,1,0:T(8,128)(2,1)S(1)} collective-permute-done((bf16[2,2,128,24,128]{4,3,2,1,0:T(8,128)(2,1)S(1)}, bf16[2,2,128,24,128]{4,3,2,1,0:T(8,128)(2,1)S(1)}, u32[]{:S(2)}, u32[]{:S(2)}) %collective-permute-start.3) | collective-permute-done | bytes 3145760 | tf_op jit(solution)/shard_map/ppermute | solution.py:16
  244.3 39.4 %collective-permute-done.4 = bf16[2,2,128,24,128]{4,3,2,1,0:T(8,128)(2,1)S(1)} collective-permute-done((bf16[2,2,128,24,128]{4,3,2,1,0:T(8,128)(2,1)S(1)}, bf16[2,2,128,24,128]{4,3,2,1,0:T(8,128)(2,1)S(1)}, u32[]{:S(2)}, u32[]{:S(2)}) %collective-permute-start.4) | collective-permute-done | bytes 3145760 | tf_op jit(solution)/shard_map/ppermute | solution.py:16
  285.3 39.5 %collective-permute-done.5 = bf16[2,2,128,24,128]{4,3,2,1,0:T(8,128)(2,1)} collective-permute-done((bf16[2,2,128,24,128]{4,3,2,1,0:T(8,128)(2,1)S(1)}, bf16[2,2,128,24,128]{4,3,2,1,0:T(8,128)(2,1)}, u32[]{:S(2)}, u32[]{:S(2)}) %collective-permute-start.5) | collective-permute-done | bytes 3145760 | tf_op jit(solution)/shard_map/ppermute | solution.py:16
  331.7 32.8 %collective-permute-done.6 = bf16[2,2,128,24,128]{4,3,2,1,0:T(8,128)(2,1)} collective-permute-done((bf16[2,2,128,24,128]{4,3,2,1,0:T(8,128)(2,1)}, bf16[2,2,128,24,128]{4,3,2,1,0:T(8,128)(2,1)}, u32[]{:S(2)}, u32[]{:S(2)}) %collective-permute-start.6) | collective-permute-done | bytes 3145760 | tf_op jit(solution)/shard_map/ppermute | solution.py:16
  384.6 126.1 %while.11 = (s32[]{:T(128)}, bf16[2,128,24,128]{1,3,2,0:T(8,128)(2,1)S(1)}, s32[2,8]{1,0:T(2,128)S(1)}, bf16[2,14,128,24,128]{4,3,2,1,0:T(8,128)(2,1)}, pred[2,8...) while((s32[]{:T(128)}, ...), condition=%wide.region_3.4_spmd.clone, body=%wide.region_0.3_spmd.clone.sunk | while | flops 1642851584 | bytes 228132912 | solution.py:79
  384.6 13.6 %gather_fusion = bf16[8,2,128,24,128]{4,3,2,1,0:T(8,128)(2,1)} fusion(bf16[2,14,128,24,128]{4,3,2,1,0:T(8,128)(2,1)} %get-tuple-element.193, s32[1024]{0:T(1024)S(1)} %pad_clamp_fusion.4), kind=kCustom, calls=%fused_computation.clone.clone.1 | custom fusion | bytes 25165856 | tf_op jit(solution)/shard_map/while/body/eval_jaxpr/gather | solution.py:59
  398.2 7.4 %copy.53 = bf16[8,2,128,24,128]{4,2,0,3,1:T(8,128)(2,1)S(1)} copy(bf16[8,2,128,24,128]{4,3,2,1,0:T(8,128)(2,1)} %gather_fusion) | data formatting | bytes 25165824 | tf_op jit(solution)/shard_map/while/body/eval_jaxpr/gather | solution.py:59
  409.2 5.5 %fusion.37 = f32[24,128,1024]{1,2,0} fusion(bf16[24,128,1024]{1,2,0:T(8,128)(2,1)S(1)} %bitcast.103, bf16[2,128,24,128]{1,3,2,0:T(8,128)(2,1)S(1)} %get-tuple-element.195, s32[]{:T(128)} %get-tuple-element.181), kind=kOutput, calls=%fused_computation.15.clone.1 | convolution fusion | flops 805306368 | bytes 19660804 | tf_op jit(solution)/shard_map/while
  414.7 6.0 %fusion.38 = (f32[24,128]{1,0:T(8,128)S(1)}, f32[24,128,8,128]{1,3,2,0:T(8,128)S(1)}) fusion(f32[24,8]{1,0:T(8,128)S(1)} %broadcast_multiply_fusion.2, pred[8]{0:T(512)(128)(4,1)S(1)} %dynamic-slice_bitcast_fusion.2, f32[24,128,1024]{1,2,0} %fusion.37), kind=kLoop, calls=%fused_computation.58.clone.1 | loop fusion | flops 12579840 | bytes 25178888 | tf_op jit(solution)/shard_map/while/body/eval_jaxpr/reduce_max | solution.py:68
  425.3 12.6 %copy.54 = f32[24,128,1024]{2,1,0:T(8,128)} copy(f32[24,128,1024]{1,2,0:T(8,128)} %bitcast.101) | data formatting | bytes 25165824 | tf_op jit(solution)/shard_map/while/body/eval_jaxpr/reshape | solution.py:65
  437.9 9.7 %fusion.39 = bf16[2,128,24,128]{1,3,2,0:T(8,128)(2,1)S(1)} fusion(bf16[2,128,24,128]{1,3,2,0:T(8,128)(2,1)S(1)} %get-tuple-element.182, s32[]{:T(128)} %get-tuple-element.181, bf16[1024,24,128]{2,0,1:T(8,128)(2,1)} %bitcast.104, f32[24,128,1024]{2,1,0:T(8,128)} %copy.54, f32[24,128]{1,0:T(8,128)S(1)} %get-tuple-element.171, f32[128,24]{0,1:T(8,128)S(1)} %bitcast.116), kind=kOutput, calls=%fused_computation.14.clone.1 | convolution fusion | flops 812384256 | bytes 19685380 | tf_op jit(solution)/shard_map/while/body/eval_jaxpr/hik,khd->ihd/dot_general | solution.py:71
  447.6 13.6 %gather_fusion = bf16[8,2,128,24,128]{4,3,2,1,0:T(8,128)(2,1)} fusion(bf16[2,14,128,24,128]{4,3,2,1,0:T(8,128)(2,1)} %get-tuple-element.193, s32[1024]{0:T(1024)S(1)} %pad_clamp_fusion.4), kind=kCustom, calls=%fused_computation.clone.clone.1 | custom fusion | bytes 25165856 | tf_op jit(solution)/shard_map/while/body/eval_jaxpr/gather | solution.py:59
  461.3 7.4 %copy.53 = bf16[8,2,128,24,128]{4,2,0,3,1:T(8,128)(2,1)S(1)} copy(bf16[8,2,128,24,128]{4,3,2,1,0:T(8,128)(2,1)} %gather_fusion) | data formatting | bytes 25165824 | tf_op jit(solution)/shard_map/while/body/eval_jaxpr/gather | solution.py:59
  472.2 5.5 %fusion.37 = f32[24,128,1024]{1,2,0} fusion(bf16[24,128,1024]{1,2,0:T(8,128)(2,1)S(1)} %bitcast.103, bf16[2,128,24,128]{1,3,2,0:T(8,128)(2,1)S(1)} %get-tuple-element.195, s32[]{:T(128)} %get-tuple-element.181), kind=kOutput, calls=%fused_computation.15.clone.1 | convolution fusion | flops 805306368 | bytes 19660804 | tf_op jit(solution)/shard_map/while
  477.8 6.0 %fusion.38 = (f32[24,128]{1,0:T(8,128)S(1)}, f32[24,128,8,128]{1,3,2,0:T(8,128)S(1)}) fusion(f32[24,8]{1,0:T(8,128)S(1)} %broadcast_multiply_fusion.2, pred[8]{0:T(512)(128)(4,1)S(1)} %dynamic-slice_bitcast_fusion.2, f32[24,128,1024]{1,2,0} %fusion.37), kind=kLoop, calls=%fused_computation.58.clone.1 | loop fusion | flops 12579840 | bytes 25178888 | tf_op jit(solution)/shard_map/while/body/eval_jaxpr/reduce_max | solution.py:68
  488.3 12.6 %copy.54 = f32[24,128,1024]{2,1,0:T(8,128)} copy(f32[24,128,1024]{1,2,0:T(8,128)} %bitcast.101) | data formatting | bytes 25165824 | tf_op jit(solution)/shard_map/while/body/eval_jaxpr/reshape | solution.py:65
  500.9 9.7 %fusion.39 = bf16[2,128,24,128]{1,3,2,0:T(8,128)(2,1)S(1)} fusion(bf16[2,128,24,128]{1,3,2,0:T(8,128)(2,1)S(1)} %get-tuple-element.182, s32[]{:T(128)} %get-tuple-element.181, bf16[1024,24,128]{2,0,1:T(8,128)(2,1)} %bitcast.104, f32[24,128,1024]{2,1,0:T(8,128)} %copy.54, f32[24,128]{1,0:T(8,128)S(1)} %get-tuple-element.171, f32[128,24]{0,1:T(8,128)S(1)} %bitcast.116), kind=kOutput, calls=%fused_computation.14.clone.1 | convolution fusion | flops 812384256 | bytes 19685380 | tf_op jit(solution)/shard_map/while/body/eval_jaxpr/hik,khd->ihd/dot_general | solution.py:71
  511.4 14.7 %all_to_all.67 = bf16[2,128,3072]{2,1,0:T(8,128)(2,1)S(1)} all-to-all(bf16[2,128,3072]{2,1,0:T(8,128)(2,1)S(1)} %copy.39), channel_id=1, replica_groups=mesh['head'=2,'blk'=16] {'head'}, dimensions={0} | all-to-all | bytes 3145728 | tf_op jit(solution)/shard_map/all_to_all | solution.py:80
  (91 shorter events, 69.1 us)
Async XLA Ops:
  0.0 330.2 %copy-start = (s32[32]{0:T(128)S(1)}, s32[32]{0:T(128)}, u32[]{:S(2)}) copy-start(s32[32]{0:T(128)} %param.13) | copy-start | bytes 388
  0.0 7.1 %copy-start.13 = (bf16[128,6144]{1,0:T(8,128)(2,1)S(1)}, bf16[128,6144]{1,0:T(8,128)(2,1)}, u32[]{:S(2)}) copy-start(bf16[128,6144]{1,0:T(8,128)(2,1)} %param.10) | copy-start | bytes 4718596
  2.8 24.4 %all-to-all-start = ((bf16[128,2,3072]{2,0,1:T(8,128)(2,1)}), bf16[128,2,3072]{2,0,1:T(8,128)(2,1)S(1)}, u32[]{:S(2)}, u32[]{:S(2)}) async-start(bf16[128,2,3072]{2,0,1:T(8,128)(2,1)} %bitcast.70), calls=%async_computation | async-start | bytes 3145728 | tf_op jit(solution)/shard_map/all_to_all | solution.py:25
  27.2 23.7 %all-to-all-start.1 = ((bf16[128,2,3072]{2,0,1:T(8,128)(2,1)}), bf16[128,2,3072]{2,0,1:T(8,128)(2,1)}, u32[]{:S(2)}, u32[]{:S(2)}) async-start(bf16[128,2,3072]{2,0,1:T(8,128)(2,1)} %bitcast.69), calls=%async_computation.1 | async-start | bytes 3145728 | tf_op jit(solution)/shard_map/all_to_all | solution.py:26
  32.2 292.6 %copy-start.14 = (bf16[128,6144]{1,0:T(8,128)(2,1)S(1)}, bf16[128,6144]{1,0:T(8,128)(2,1)}, u32[]{:S(2)}) copy-start(bf16[128,6144]{1,0:T(8,128)(2,1)} %param.8) | copy-start | bytes 4718596
  53.8 276.2 %copy-start.16 = (s32[2,8]{1,0:T(2,128)S(1)}, s32[2,8]{1,0:T(2,128)}, u32[]{:S(2)}) copy-start(s32[2,8]{1,0:T(2,128)} %param.11) | copy-start | bytes 196
  53.8 277.8 %copy-start.17 = (s32[2]{0:T(128)S(1)}, s32[2]{0:T(128)}, u32[]{:S(2)}) copy-start(s32[2]{0:T(128)} %param.12) | copy-start | bytes 28
  54.1 66.9 %collective-permute-start = (bf16[2,2,128,24,128]{4,3,2,1,0:T(8,128)(2,1)S(1)}, bf16[2,2,128,24,128]{4,3,2,1,0:T(8,128)(2,1)S(1)}, u32[]{:S(2)}, u32[]{:S(2)}) collective-permute-start(bf16[2,2,128,24,128]{4,3,2,1,0:T(8,128)(2,1)S(1)} %pad_maximum_fusion), channel_id=1, source_target_pairs={{3,0},{4,1},{5,2},{6,3},{7,4},{8,5},{9,6},{10,7},{11,8},{12,9},{13... | collective-permute-start | bytes 9437192 | tf_op jit(solution)/shard_map/ppermute | solution.py:16
  122.7 39.4 %collective-permute-start.1 = (bf16[2,2,128,24,128]{4,3,2,1,0:T(8,128)(2,1)S(1)}, bf16[2,2,128,24,128]{4,3,2,1,0:T(8,128)(2,1)S(1)}, u32[]{:S(2)}, u32[]{:S(2)}) collective-permute-start(bf16[2,2,128,24,128]{4,3,2,1,0:T(8,128)(2,1)S(1)} %collective-permute-done), channel_id=1, source_target_pairs={{15,0},{0,1},{1,2},{2,3},{3,4},{4,5},{5,6},{6,7},{7,8},{8,9},{9,10... | collective-permute-start | bytes 9437192 | tf_op jit(solution)/shard_map/ppermute | solution.py:16
  163.8 39.4 %collective-permute-start.2 = (bf16[2,2,128,24,128]{4,3,2,1,0:T(8,128)(2,1)S(1)}, bf16[2,2,128,24,128]{4,3,2,1,0:T(8,128)(2,1)S(1)}, u32[]{:S(2)}, u32[]{:S(2)}) collective-permute-start(bf16[2,2,128,24,128]{4,3,2,1,0:T(8,128)(2,1)S(1)} %collective-permute-done.1), channel_id=1, source_target_pairs={{15,0},{0,1},{1,2},{2,3},{3,4},{4,5},{5,6},{6,7},{7,8},{8,9},{9,10... | collective-permute-start | bytes 9437192 | tf_op jit(solution)/shard_map/ppermute | solution.py:16
  204.9 39.4 %collective-permute-start.3 = (bf16[2,2,128,24,128]{4,3,2,1,0:T(8,128)(2,1)S(1)}, bf16[2,2,128,24,128]{4,3,2,1,0:T(8,128)(2,1)S(1)}, u32[]{:S(2)}, u32[]{:S(2)}) collective-permute-start(bf16[2,2,128,24,128]{4,3,2,1,0:T(8,128)(2,1)S(1)} %collective-permute-done.2), channel_id=1, source_target_pairs={{15,0},{0,1},{1,2},{2,3},{3,4},{4,5},{5,6},{6,7},{7,8},{8,9},{9,10... | collective-permute-start | bytes 9437192 | tf_op jit(solution)/shard_map/ppermute | solution.py:16
  244.3 39.4 %collective-permute-start.4 = (bf16[2,2,128,24,128]{4,3,2,1,0:T(8,128)(2,1)S(1)}, bf16[2,2,128,24,128]{4,3,2,1,0:T(8,128)(2,1)S(1)}, u32[]{:S(2)}, u32[]{:S(2)}) collective-permute-start(bf16[2,2,128,24,128]{4,3,2,1,0:T(8,128)(2,1)S(1)} %collective-permute-done.3), channel_id=1, source_target_pairs={{15,0},{0,1},{1,2},{2,3},{3,4},{4,5},{5,6},{6,7},{7,8},{8,9},{9,10... | collective-permute-start | bytes 9437192 | tf_op jit(solution)/shard_map/ppermute | solution.py:16
  285.3 39.5 %collective-permute-start.5 = (bf16[2,2,128,24,128]{4,3,2,1,0:T(8,128)(2,1)S(1)}, bf16[2,2,128,24,128]{4,3,2,1,0:T(8,128)(2,1)}, u32[]{:S(2)}, u32[]{:S(2)}) collective-permute-start(bf16[2,2,128,24,128]{4,3,2,1,0:T(8,128)(2,1)S(1)} %collective-permute-done.4), channel_id=1, source_target_pairs={{15,0},{0,1},{1,2},{2,3},{3,4},{4,5},{5,6},{6,7},{7,8},{8,9},{9,10... | collective-permute-start | bytes 9437192 | tf_op jit(solution)/shard_map/ppermute | solution.py:16
  324.8 39.7 %collective-permute-start.6 = (bf16[2,2,128,24,128]{4,3,2,1,0:T(8,128)(2,1)}, bf16[2,2,128,24,128]{4,3,2,1,0:T(8,128)(2,1)}, u32[]{:S(2)}, u32[]{:S(2)}) collective-permute-start(bf16[2,2,128,24,128]{4,3,2,1,0:T(8,128)(2,1)} %collective-permute-done.5), channel_id=1, source_target_pairs={{15,0},{0,1},{1,2},{2,3},{3,4},{4,5},{5,6},{6,7},{7,8},{8,9},{9,10... | collective-permute-start | bytes 9437192 | tf_op jit(solution)/shard_map/ppermute | solution.py:16
  326.3 58.2 %all-to-all-start.2 = ((bf16[128,2,3072]{0,2,1:T(8,128)(2,1)}), bf16[128,2,3072]{0,2,1:T(8,128)(2,1)S(1)}, u32[]{:S(2)}, u32[]{:S(2)}) async-start(bf16[128,2,3072]{0,2,1:T(8,128)(2,1)} %bitcast.110), calls=%async_computation.2 | async-start | bytes 3145728 | tf_op jit(solution)/shard_map/all_to_all | solution.py:24
  331.7 41.0 %copy-start.12 = (bf16[2,2,128,24,128]{4,3,2,1,0:T(8,128)(2,1)S(1)}, bf16[2,2,128,24,128]{4,3,2,1,0:T(8,128)(2,1)}, u32[]{:S(2)}) copy-start(bf16[2,2,128,24,128]{4,3,2,1,0:T(8,128)(2,1)} %copy-done.11) | copy-start | bytes 9437188
  372.7 3.7 copy-start.4
  372.7 5.1 copy-start.10
  374.9 5.1 copy-start.8
  377.8 4.5 copy-start.6
  380.1 4.5 copy-start.15
  420.7 4.6 copy-start.2
  483.8 4.6 copy-start.2
  510.7 17.9 %copy-start.1 = (s32[32]{0:T(128)S(1)}, s32[32]{0:T(128)}, u32[]{:S(2)}) copy-start(s32[32]{0:T(128)} %param.13) | copy-start | bytes 388
  (5 other events, 7.9 us)
where the time goes:
time: 530 us; the launch traced here: 529 us
  waiting for transfers between devices  330 us (62%)
  local copies, waits for them, and re-layouts  120 us (23%)
  matrix products  30.4 us (6%)
  starting transfers between devices  16.6 us (3%)
  other arithmetic  16.5 us (3%)
  blocking collectives  14.7 us (3%)
    ppermute x7, waiting for transfers between devices, shifted(): return lax.ppermute(block, axis, route)  293 us
    gather x4, local copies, waits for them, and re-layouts, one_tile(): chosen = window[:, where_index]  42.1 us
    unnamed x44, local copies, waits for them, and re-layouts  29.3 us
    reshape x2, local copies, waits for them, and re-layouts, one_tile(): jnp.where(valid_row[None, None, :, None], scores, -1e+30)  25.1 us
    dot_general x2, matrix products, one_tile(): jnp.einsum('hik,khd->ihd', weights, chosen[1].reshape(SLOTS * TILE, heads...  19.5 us
    all_to_all x1, waiting for transfers between devices, body(): lax.all_to_all(key_states, 'head', split_axis=1, concat_axis=0, tiled=True)  18.9 us
    all_to_all x1, waiting for transfers between devices, body(): lax.all_to_all(value_states, 'head', split_axis=1, concat_axis=0, tiled=T...  18.7 us
    all_to_all x1, blocking collectives, body(): lax.all_to_all(out_tiles.reshape(shard_tok, heads_local * DH), 'head', sp...  14.7 us
  transfers between devices with their start and end apart: 10, of which 9 were waited for; matrix products, arithmetic and copies ran while one was open for 5% of the time, Pallas kernels for 0%

commit v1 on v0

v1 whole, which is shorter than its diff:
```python
import functools

import jax
import jax.numpy as jnp
import numpy as np
from jax import lax
from jax.experimental import pallas as pl
from jax.experimental.pallas import tpu as pltpu
from jax.sharding import PartitionSpec as P

H = 48
DH = 128
TILE = 128
REACH = 3
SLOTS = 8
GROUP = 8
HEADS = H // GROUP
META_ROWS = 8
MESH = pl.DeviceIdType.MESH


def kernel(
    blk_size,
    head_size,
    q_ref,
    k_ref,
    v_ref,
    meta_ref,
    order_ref,
    slope_ref,
    out_ref,
    *scratch,
):
    kv_bufs = scratch[:HEADS]
    (q_buf, o_buf, meta_v, meta_s, send_sem, near_sem, q_sem, far_sem, far_send_sem, out_send_sem, out_sem, meta_sem) = scratch[HEADS:]
    members = GROUP // head_size
    tps = head_size
    groups = blk_size // members
    side = REACH * tps
    hops = -(-REACH // members)

    blk = lax.axis_index("blk")
    head = lax.axis_index("head")
    group = blk // members
    place = blk % members
    mine = place * head_size + head

    def in_group(p):
        return {"blk": group * members + p // head_size, "head": p % head_size}

    def group_at(distance):
        return {"blk": (group + distance + groups) % groups * members + place, "head": head}

    far = []
    for hop in range(1, hops + 1):
        start = max(0, hop * members - REACH)
        far.append((hop, start * tps, (members - start) * tps, (start - hop * members + REACH) * tps))
        count = min(members, REACH - (hop - 1) * members)
        far.append((-hop, 0, count * tps, (hop * members + REACH) * tps))

    barrier = pltpu.get_barrier_semaphore()

    def greet(k, carry):
        pl.semaphore_signal(barrier, inc=1, device_id=in_group((mine + k) % GROUP), device_id_type=MESH)
        return carry

    lax.fori_loop(1, GROUP, greet, 0)
    for distance, *_ in far:
        pl.semaphore_signal(barrier, inc=1, device_id=group_at(distance), device_id_type=MESH)
    pl.semaphore_wait(barrier, GROUP - 1 + len(far))

    pltpu.make_async_copy(meta_ref, meta_v.at[place], meta_sem.at[0]).start()
    for k in range(1, members):
        pltpu.make_async_remote_copy(
            src_ref=meta_ref,
            dst_ref=meta_v.at[place],
            send_sem=meta_sem.at[1],
            recv_sem=meta_sem.at[0],
            device_id={"blk": group * members + (place + k) % members, "head": head},
            device_id_type=MESH,
        ).start()

    def columns(p, chunk):
        return pl.ds(pl.multiple_of((p * HEADS + chunk) * DH, DH), DH)

    def scatter(chunk, parts):
        for source, target, send, recv in parts:
            pltpu.make_async_copy(source.at[:, columns(mine, chunk)], target, recv).start()

        def to_peer(k, carry):
            p = (mine + k) % GROUP
            for source, target, send, recv in parts:
                pltpu.make_async_remote_copy(
                    src_ref=source.at[:, columns(p, chunk)],
                    dst_ref=target,
                    send_sem=send,
                    recv_sem=recv,
                    device_id=in_group(p),
                    device_id_type=MESH,
                ).start()
            return carry

        lax.fori_loop(1, GROUP, to_peer, 0)

    for chunk in range(HEADS):
        scatter(
            chunk,
            (
                (k_ref, kv_bufs[chunk].at[0, side + mine], send_sem.at[0], near_sem.at[chunk]),
                (v_ref, kv_bufs[chunk].at[1, side + mine], send_sem.at[1], near_sem.at[chunk]),
            ),
        )
    for chunk in range(HEADS):
        scatter(chunk, ((q_ref, q_buf.at[chunk, mine], send_sem.at[2], q_sem.at[chunk]),))

    for chunk in range(HEADS):
        own = kv_bufs[chunk].at[:, pl.ds(side, GROUP)]
        pltpu.make_async_copy(own, own, near_sem.at[chunk]).wait()
        for distance, first, tiles, there in far:
            pltpu.make_async_remote_copy(
                src_ref=kv_bufs[chunk].at[:, pl.ds(side + first, tiles)],
                dst_ref=kv_bufs[chunk].at[:, pl.ds(there, tiles)],
                send_sem=far_send_sem.at[chunk],
                recv_sem=far_sem.at[chunk],
                device_id=group_at(distance),
                device_id_type=MESH,
            ).start()

    pltpu.make_async_copy(meta_v, meta_v, meta_sem.at[0]).wait()
    to_scalar = pltpu.make_async_copy(meta_v, meta_s, meta_sem.at[2])
    to_scalar.start()
    to_scalar.wait()

    ones = jnp.ones((2 * TILE, DH), jnp.bfloat16)
    ntiles = order_ref.shape[0]
    scale = DH ** (-0.5)

    def attend(chunk):
        kv = kv_bufs[chunk]
        slope = slope_ref[mine * HEADS + chunk]

        def one_tile(k, carry):
            i = (mine + k) % GROUP
            q = q_buf[chunk, i]
            member, row = i // tps, i % tps
            count = meta_s[member, row, SLOTS]
            here = order_ref[group * GROUP + i]
            scores, values = [], []
            for c in range(SLOTS):
                u = meta_s[member, row, c]
                index = (u // tps - group * members + REACH + blk_size) % blk_size * tps + u % tps
                index = jnp.minimum(index, kv.shape[1] - 1)
                distance = jnp.abs(here - order_ref[u]).astype(jnp.float32) * (1.0 / ntiles)
                bias = jnp.where(c < count, slope * distance, 1e30)
                dots = lax.dot_general(
                    q, kv[0, index], (((1,), (1,)), ((), ())), preferred_element_type=jnp.float32
                )
                scores.append(dots * scale - bias)
                values.append(kv[1, index])
            top = functools.reduce(jnp.maximum, scores)
            top = jnp.max(top, axis=1, keepdims=True)
            mixed = jnp.zeros((TILE, 2 * DH), jnp.float32)
            for c in range(0, SLOTS, 2):
                weights = jnp.concatenate(
                    [jnp.exp(scores[c + e] - top).astype(jnp.bfloat16) for e in (0, 1)], axis=1
                )
                pair = jnp.concatenate([values[c], values[c + 1]], axis=0)
                mixed += jnp.dot(
                    weights,
                    jnp.concatenate([pair, ones], axis=1),
                    preferred_element_type=jnp.float32,
                )
            o_buf[chunk, i] = (mixed[:, :DH] / mixed[:, DH:]).astype(jnp.bfloat16)
            target = out_ref.at[:, columns(mine, chunk)]

            @pl.when(i == mine)
            def _():
                pltpu.make_async_copy(o_buf.at[chunk, i], target, out_sem).start()

            @pl.when(i != mine)
            def _():
                pltpu.make_async_remote_copy(
                    src_ref=o_buf.at[chunk, i],
                    dst_ref=target,
                    send_sem=out_send_sem,
                    recv_sem=out_sem,
                    device_id=in_group(i),
                    device_id_type=MESH,
                ).start()

            return carry

        lax.fori_loop(1, GROUP + 1, one_tile, 0)

    for chunk in range(HEADS):
        arrived = kv_bufs[chunk].at[:, pl.ds(0, 2 * side)]
        pltpu.make_async_copy(arrived, arrived, far_sem.at[chunk]).wait()
        pltpu.make_async_copy(q_buf.at[chunk], q_buf.at[chunk], q_sem.at[chunk]).wait()
        attend(chunk)

    sent = (GROUP - 1) * HEADS * DH
    for which, source in enumerate((k_ref, v_ref, q_ref)):
        part = source.at[:, pl.ds(0, sent)]
        pltpu.make_async_copy(part, part, send_sem.at[which]).wait()
    if members > 1:
        part = meta_v.at[pl.ds(0, members - 1)]
        pltpu.make_async_copy(part, part, meta_sem.at[1]).wait()
    for chunk in range(HEADS):
        arrived = kv_bufs[chunk].at[:, pl.ds(0, 2 * side)]
        pltpu.make_async_copy(arrived, arrived, far_send_sem.at[chunk]).wait()
    part = out_ref.at[:, pl.ds(0, sent)]
    pltpu.make_async_copy(part, part, out_send_sem).wait()
    pltpu.make_async_copy(out_ref, out_ref, out_sem).wait()


def body(queries, key_states, value_states, block_lists, block_counts, tile_order):
    blk_size = lax.axis_size("blk")
    head_size = lax.axis_size("head")
    members = GROUP // head_size
    window = GROUP + 2 * REACH * head_size
    meta = jnp.concatenate((block_lists, block_counts[:, None]), axis=1)
    meta = jnp.pad(meta, ((0, META_ROWS - meta.shape[0]), (0, 128 - meta.shape[1])))
    slopes = jnp.asarray(8.0 * 2.0 ** (-8.0 * np.arange(H) / H), jnp.float32)
    hbm = pl.BlockSpec(memory_space=pl.ANY)
    smem = pl.BlockSpec(memory_space=pltpu.SMEM)
    dma = pltpu.SemaphoreType.DMA
    return pl.pallas_call(
        functools.partial(kernel, blk_size, head_size),
        out_shape=jax.ShapeDtypeStruct(queries.shape, jnp.bfloat16),
        in_specs=[hbm, hbm, hbm, hbm, smem, smem],
        out_specs=hbm,
        scratch_shapes=[pltpu.VMEM((2, window, TILE, DH), jnp.bfloat16) for _ in range(HEADS)]
        + [
            pltpu.VMEM((HEADS, GROUP, TILE, DH), jnp.bfloat16),
            pltpu.VMEM((HEADS, GROUP, TILE, DH), jnp.bfloat16),
            pltpu.VMEM((members, META_ROWS, 128), jnp.int32),
            pltpu.SMEM((members, META_ROWS, 128), jnp.int32),
            dma((3,)),
            dma((HEADS,)),
            dma((HEADS,)),
            dma((HEADS,)),
            dma((HEADS,)),
            dma,
            dma,
            dma((3,)),
        ],
        compiler_params=pltpu.CompilerParams(
            collective_id=0, has_side_effects=True, vmem_limit_bytes=50 * 2**20
        ),
        cost_estimate=pl.CostEstimate(
            flops=4 * GROUP * HEADS * SLOTS * TILE * TILE * DH,
            bytes_accessed=8 * queries.size,
            transcendentals=GROUP * HEADS * SLOTS * TILE * TILE,
        ),
    )(queries, key_states, value_states, meta, tile_order, slopes)


def solution(mesh):
    in_specs = (
        P(("blk", "head"), None),
        P(("blk", "head"), None),
        P(("blk", "head"), None),
        P("blk", None),
        P("blk"),
        P(),
    )
    out_specs = P(("blk", "head"), None)
    return jax.shard_map(body, mesh=mesh, in_specs=in_specs, out_specs=out_specs, check_vma=False)
```

time: 530 us -> 129 us (0.24)
  waiting for transfers between devices: 330 us -> 0 us
  Pallas kernels: 0 us -> 123 us
  local copies, waits for them, and re-layouts: 120 us -> 4.61 us
  matrix products: 30.4 us -> 0 us
  starting transfers between devices: 16.6 us -> 0 us
  other arithmetic: 16.5 us -> 0.75 us
  blocking collectives: 14.7 us -> 0 us
    ppermute x7 -> x0, waiting for transfers between devices: 293 us -> none  [shifted(): return lax.ppermute(block, axis, route)]
    pallas_call x0 -> x1, Pallas kernels: none -> 123 us  [body(): pl.pallas_call(functools.partial(kernel, blk_size, head_size), out_shape=...]
    gather x7 -> x0, local copies, waits for them, and re-layouts: 43.5 us -> none  [the longest x4 42.1 us: one_tile(): chosen = window[:, where_index]]
    all_to_all x3 -> x0, waiting for transfers between devices: 37.6 us -> none  [the longest x1 18.9 us: body(): lax.all_to_all(key_states, 'head', split_axis=1, concat_axis=0, tiled=True)]
    unnamed x44 -> x7, local copies, waits for them, and re-layouts: 29.3 us -> 3.86 us
    reshape x2 -> x0, local copies, waits for them, and re-layouts: 25.1 us -> none  [one_tile(): jnp.where(valid_row[None, None, :, None], scores, -1e+30)]
    dot_general x2 -> x0, matrix products: 19.5 us -> none  [one_tile(): jnp.einsum('hik,khd->ihd', weights, chosen[1].reshape(SLOTS * TILE, heads...]
    all_to_all x1 -> x0, blocking collectives: 14.7 us -> none  [body(): lax.all_to_all(out_tiles.reshape(shard_tok, heads_local * DH), 'head', sp...]
  transfers between devices with their start and end apart: 10 -> 0, of which waited for: 9 -> 0; matrix products, arithmetic and copies ran while one was open for 5% -> 0% of each run, Pallas kernels for 0% -> 0%
where the time goes in v1:
time: 129 us; the launch traced here: 128 us
  Pallas kernels  123 us (95%)
  local copies, waits for them, and re-layouts  4.61 us (4%)
    pallas_call x1, Pallas kernels, body(): pl.pallas_call(functools.partial(kernel, blk_size, head_size), out_shape=...  123 us
    unnamed x7, local copies, waits for them, and re-layouts  3.86 us

profile of v1, /device:TPU:0, one launch (start us, length us, event | category | flops | bytes accessed | tf_op | source)
XLA Modules:
  0.0 128.2 jit_solution(1031075182559235326)
XLA Ops:
  0.0 0.7 copy.8
  0.7 0.8 pad_add_fusion
  1.5 0.0 copy-start
  1.5 1.4 %copy-done = bf16[128,6144]{1,0:T(8,128)(2,1)S(1)} copy-done((bf16[128,6144]{1,0:T(8,128)(2,1)S(1)}, bf16[128,6144]{1,0:T(8,128)(2,1)}, u32[]{:S(2)}) %copy-start) | copy-done | bytes 1572888
  2.9 0.0 copy-start.1
  2.9 0.7 copy-done.1
  3.6 0.0 copy-start.2
  3.6 0.7 copy-done.2
  4.2 122.9 %shard_map.73 = bf16[128,6144]{1,0:T(8,128)(2,1)S(1)} custom-call(bf16[128,6144]{1,0:T(8,128)(2,1)S(1)} %copy-done, bf16[128,6144]{1,0:T(8,128)(2,1)} %k_ref.1, bf16[128,6144]{1,0:T(8,128)(2,1)} %v_ref.1, s32[8,128]{1,0:T(8,128)S(1)} %pad.4.meta_ref, s32[32]{0:T(128)S(1)} %copy-done.1, f32[48]{0:T(128)S(1)} %copy-done.2), custom_call_target="tpu_custom_call" | custom-call | flops 3221225472 | bytes 6291456 | tf_op jit(solution)/shard_map/pallas_call | solution.py:227
  127.1 1.1 copy.10
  (1 shorter events, 0.0 us)
Async XLA Ops:
  1.5 1.4 %copy-start = (bf16[128,6144]{1,0:T(8,128)(2,1)S(1)}, bf16[128,6144]{1,0:T(8,128)(2,1)}, u32[]{:S(2)}) copy-start(bf16[128,6144]{1,0:T(8,128)(2,1)} %q_ref.1) | copy-start | bytes 4718596
  2.9 0.7 copy-start.1
  3.6 0.7 copy-start.2

commit v2 on v1

--- a/solution.py
+++ b/solution.py
@@ -2,7 +2,6 @@
 
 import jax
 import jax.numpy as jnp
-import numpy as np
 from jax import lax
 from jax.experimental import pallas as pl
 from jax.experimental.pallas import tpu as pltpu
@@ -25,9 +24,9 @@
     q_ref,
     k_ref,
     v_ref,
-    meta_ref,
+    lists_ref,
+    counts_ref,
     order_ref,
-    slope_ref,
     out_ref,
     *scratch,
 ):
@@ -69,10 +68,17 @@
         pl.semaphore_signal(barrier, inc=1, device_id=group_at(distance), device_id_type=MESH)
     pl.semaphore_wait(barrier, GROUP - 1 + len(far))
 
-    pltpu.make_async_copy(meta_ref, meta_v.at[place], meta_sem.at[0]).start()
+    rows = lax.broadcasted_iota(jnp.int32, (META_ROWS, 128), 0)
+    lanes = lax.broadcasted_iota(jnp.int32, (META_ROWS, 128), 1)
+    meta = jnp.zeros((META_ROWS, 128), jnp.int32)
+    for r in range(tps):
+        for c in range(SLOTS + 1):
+            item = lists_ref[r, c] if c < SLOTS else counts_ref[r]
+            meta = jnp.where((rows == r) & (lanes == c), item, meta)
+    meta_v[place] = meta
     for k in range(1, members):
         pltpu.make_async_remote_copy(
-            src_ref=meta_ref,
+            src_ref=meta_v.at[place],
             dst_ref=meta_v.at[place],
             send_sem=meta_sem.at[1],
             recv_sem=meta_sem.at[0],
@@ -102,7 +108,23 @@
 
         lax.fori_loop(1, GROUP, to_peer, 0)
 
+    def own_tile(chunk):
+        for distance, first, tiles, there in far:
+
+            @pl.when((mine >= first) & (mine < first + tiles))
+            def _():
+                for e, source in enumerate((k_ref, v_ref)):
+                    pltpu.make_async_remote_copy(
+                        src_ref=source.at[:, columns(mine, chunk)],
+                        dst_ref=kv_bufs[chunk].at[e, there - first + mine],
+                        send_sem=far_send_sem.at[chunk],
+                        recv_sem=far_sem.at[chunk],
+                        device_id=group_at(distance),
+                        device_id_type=MESH,
+                    ).start()
+
     for chunk in range(HEADS):
+        own_tile(chunk)
         scatter(
             chunk,
             (
@@ -111,22 +133,32 @@
             ),
         )
     for chunk in range(HEADS):
-        scatter(chunk, ((q_ref, q_buf.at[chunk, mine], send_sem.at[2], q_sem.at[chunk]),))
-
-    for chunk in range(HEADS):
         own = kv_bufs[chunk].at[:, pl.ds(side, GROUP)]
         pltpu.make_async_copy(own, own, near_sem.at[chunk]).wait()
-        for distance, first, tiles, there in far:
-            pltpu.make_async_remote_copy(
-                src_ref=kv_bufs[chunk].at[:, pl.ds(side + first, tiles)],
-                dst_ref=kv_bufs[chunk].at[:, pl.ds(there, tiles)],
-                send_sem=far_send_sem.at[chunk],
-                recv_sem=far_sem.at[chunk],
-                device_id=group_at(distance),
-                device_id_type=MESH,
-            ).start()
-
-    pltpu.make_async_copy(meta_v, meta_v, meta_sem.at[0]).wait()
+
+        def pass_on(k, carry):
+            p = (mine + k) % GROUP
+            for distance, first, tiles, there in far:
+
+                @pl.when((p >= first) & (p < first + tiles))
+                def _():
+                    pltpu.make_async_remote_copy(
+                        src_ref=kv_bufs[chunk].at[:, side + p],
+                        dst_ref=kv_bufs[chunk].at[:, there - first + p],
+                        send_sem=far_send_sem.at[chunk],
+                        recv_sem=far_sem.at[chunk],
+                        device_id=group_at(distance),
+                        device_id_type=MESH,
+                    ).start()
+
+            return carry
+
+        lax.fori_loop(1, GROUP, pass_on, 0)
+        scatter(chunk, ((q_ref, q_buf.at[chunk, mine], send_sem.at[2], q_sem.at[chunk]),))
+
+    if members > 1:
+        part = meta_v.at[pl.ds(0, members - 1)]
+        pltpu.make_async_copy(part, part, meta_sem.at[0]).wait()
     to_scalar = pltpu.make_async_copy(meta_v, meta_s, meta_sem.at[2])
     to_scalar.start()
     to_scalar.wait()
@@ -137,26 +169,30 @@
 
     def attend(chunk):
         kv = kv_bufs[chunk]
-        slope = slope_ref[mine * HEADS + chunk]
-
-        def one_tile(k, carry):
-            i = (mine + k) % GROUP
+        slope = (1 << (GROUP - 1 - mine)).astype(jnp.float32) * (
+            8.0 * 2.0 ** (-8.0 * chunk / H) / 2 ** (GROUP - 1) / ntiles
+        )
+
+        def one_tile(i):
             q = q_buf[chunk, i]
             member, row = i // tps, i % tps
             count = meta_s[member, row, SLOTS]
             here = order_ref[group * GROUP + i]
-            scores, values = [], []
+            places, biases = [], []
             for c in range(SLOTS):
                 u = meta_s[member, row, c]
                 index = (u // tps - group * members + REACH + blk_size) % blk_size * tps + u % tps
-                index = jnp.minimum(index, kv.shape[1] - 1)
-                distance = jnp.abs(here - order_ref[u]).astype(jnp.float32) * (1.0 / ntiles)
-                bias = jnp.where(c < count, slope * distance, 1e30)
+                places.append(jnp.minimum(index, kv.shape[1] - 1))
+                distance = jnp.abs(here - order_ref[u]).astype(jnp.float32)
+                biases.append(jnp.where(c < count, slope * distance, 1e30))
+            scores = []
+            for c in range(0, SLOTS, 2):
+                pair = jnp.concatenate([kv[0, places[c]], kv[0, places[c + 1]]], axis=0)
                 dots = lax.dot_general(
-                    q, kv[0, index], (((1,), (1,)), ((), ())), preferred_element_type=jnp.float32
+                    q, pair, (((1,), (1,)), ((), ())), preferred_element_type=jnp.float32
                 )
-                scores.append(dots * scale - bias)
-                values.append(kv[1, index])
+                for e in (0, 1):
+                    scores.append(dots[:, e * TILE : (e + 1) * TILE] * scale - biases[c + e])
             top = functools.reduce(jnp.maximum, scores)
             top = jnp.max(top, axis=1, keepdims=True)
             mixed = jnp.zeros((TILE, 2 * DH), jnp.float32)
@@ -164,15 +200,17 @@
                 weights = jnp.concatenate(
                     [jnp.exp(scores[c + e] - top).astype(jnp.bfloat16) for e in (0, 1)], axis=1
                 )
-                pair = jnp.concatenate([values[c], values[c + 1]], axis=0)
+                pair = jnp.concatenate([kv[1, places[c]], kv[1, places[c + 1]]], axis=0)
                 mixed += jnp.dot(
                     weights,
                     jnp.concatenate([pair, ones], axis=1),
                     preferred_element_type=jnp.float32,
                 )
-            o_buf[chunk, i] = (mixed[:, :DH] / mixed[:, DH:]).astype(jnp.bfloat16)
-            target = out_ref.at[:, columns(mine, chunk)]
-
+            return (mixed[:, :DH] / mixed[:, DH:]).astype(jnp.bfloat16)
+
+        target = out_ref.at[:, columns(mine, chunk)]
+
+        def send(i):
             @pl.when(i == mine)
             def _():
                 pltpu.make_async_copy(o_buf.at[chunk, i], target, out_sem).start()
@@ -188,9 +226,16 @@
                     device_id_type=MESH,
                 ).start()
 
+        def two_tiles(k, carry):
+            pair = [(mine + 1 + 2 * k + e) % GROUP for e in (0, 1)]
+            results = [one_tile(i) for i in pair]
+            for i, result in zip(pair, results):
+                o_buf[chunk, i] = result
+            for i in pair:
+                send(i)
             return carry
 
-        lax.fori_loop(1, GROUP + 1, one_tile, 0)
+        lax.fori_loop(0, GROUP // 2, two_tiles, 0)
 
     for chunk in range(HEADS):
         arrived = kv_bufs[chunk].at[:, pl.ds(0, 2 * side)]
@@ -218,16 +263,13 @@
     head_size = lax.axis_size("head")
     members = GROUP // head_size
     window = GROUP + 2 * REACH * head_size
-    meta = jnp.concatenate((block_lists, block_counts[:, None]), axis=1)
-    meta = jnp.pad(meta, ((0, META_ROWS - meta.shape[0]), (0, 128 - meta.shape[1])))
-    slopes = jnp.asarray(8.0 * 2.0 ** (-8.0 * np.arange(H) / H), jnp.float32)
     hbm = pl.BlockSpec(memory_space=pl.ANY)
     smem = pl.BlockSpec(memory_space=pltpu.SMEM)
     dma = pltpu.SemaphoreType.DMA
     return pl.pallas_call(
         functools.partial(kernel, blk_size, head_size),
         out_shape=jax.ShapeDtypeStruct(queries.shape, jnp.bfloat16),
-        in_specs=[hbm, hbm, hbm, hbm, smem, smem],
+        in_specs=[hbm, hbm, hbm, smem, smem, smem],
         out_specs=hbm,
         scratch_shapes=[pltpu.VMEM((2, window, TILE, DH), jnp.bfloat16) for _ in range(HEADS)]
         + [
@@ -245,14 +287,14 @@
             dma((3,)),
         ],
         compiler_params=pltpu.CompilerParams(
-            collective_id=0, has_side_effects=True, vmem_limit_bytes=50 * 2**20
+            collective_id=0, has_side_effects=True, vmem_limit_bytes=63 * 2**20
         ),
         cost_estimate=pl.CostEstimate(
             flops=4 * GROUP * HEADS * SLOTS * TILE * TILE * DH,
             bytes_accessed=8 * queries.size,
             transcendentals=GROUP * HEADS * SLOTS * TILE * TILE,
         ),
-    )(queries, key_states, value_states, meta, tile_order, slopes)
+    )(queries, key_states, value_states, block_lists, block_counts, tile_order)
 
 
 def solution(mesh):

time: 129 us -> 119 us (0.922)
  Pallas kernels: 123 us -> 116 us
  local copies, waits for them, and re-layouts: 4.61 us -> 2.69 us
    pallas_call x1, Pallas kernels: 123 us -> 116 us  [body(): pl.pallas_call(functools.partial(kernel, blk_size, head_size), out_shape=...]
    unnamed x7 -> x1, local copies, waits for them, and re-layouts: 3.86 us -> 2.69 us
where the time goes in v2:
time: 119 us
  Pallas kernels  116 us (97%)
  local copies, waits for them, and re-layouts  2.69 us (2%)
    pallas_call x1, Pallas kernels, body(): pl.pallas_call(functools.partial(kernel, blk_size, head_size), out_shape=...  116 us
    unnamed x1, local copies, waits for them, and re-layouts  2.69 us

profile of v2, /device:TPU:0, one launch (start us, length us, event | category | flops | bytes accessed | tf_op | source)
XLA Modules:
  0.0 119.0 jit_solution(2007089709632365003)
XLA Ops:
  0.0 116.3 %shard_map.64 = bf16[128,6144]{1,0:T(8,128)(2,1)} custom-call(bf16[128,6144]{1,0:T(8,128)(2,1)} %q_ref.1, bf16[128,6144]{1,0:T(8,128)(2,1)} %k_ref.1, bf16[128,6144]{1,0:T(8,128)(2,1)} %v_ref.1, s32[2,8]{1,0:T(2,128)} %lists_ref.1, s32[2]{0:T(128)} %counts_ref.1, s32[32]{0:T(128)} %order_ref.1), custom_call_target="tpu_custom_call" | custom-call | flops 3221225472 | bytes 6291456 | tf_op jit(solution)/shard_map/pallas_call | solution.py:269
  116.3 2.7 %copy.8 = bf16[128,6144]{1,0:T(8,128)(2,1)} copy(bf16[128,6144]{1,0:T(8,128)(2,1)} %shard_map.64) | data formatting | bytes 3145728

commit v3 on v2

--- a/solution.py
+++ b/solution.py
@@ -30,8 +30,8 @@
     out_ref,
     *scratch,
 ):
-    kv_bufs = scratch[:HEADS]
-    (q_buf, o_buf, meta_v, meta_s, send_sem, near_sem, q_sem, far_sem, far_send_sem, out_send_sem, out_sem, meta_sem) = scratch[HEADS:]
+    kv_bufs = [(ref,) for ref in scratch[: HEADS - 1]] + [scratch[HEADS - 1 : HEADS + 1]]
+    (q_buf, o_buf, w_buf, meta_v, meta_s, send_sem, near_sem, q_sem, far_sem, far_send_sem, out_send_sem, out_sem, meta_sem) = scratch[HEADS + 1 :]
     members = GROUP // head_size
     tps = head_size
     groups = blk_size // members
@@ -86,6 +86,13 @@
             device_id_type=MESH,
         ).start()
 
+    def half(chunk, e):
+        bufs = kv_bufs[chunk]
+        return bufs[0].at[e] if len(bufs) == 1 else bufs[e].at[0]
+
+    def sem_of(chunk, e):
+        return chunk + e if len(kv_bufs[chunk]) > 1 else chunk
+
     def columns(p, chunk):
         return pl.ds(pl.multiple_of((p * HEADS + chunk) * DH, DH), DH)
 
@@ -116,9 +123,9 @@
                 for e, source in enumerate((k_ref, v_ref)):
                     pltpu.make_async_remote_copy(
                         src_ref=source.at[:, columns(mine, chunk)],
-                        dst_ref=kv_bufs[chunk].at[e, there - first + mine],
-                        send_sem=far_send_sem.at[chunk],
-                        recv_sem=far_sem.at[chunk],
+                        dst_ref=half(chunk, e).at[there - first + mine],
+                        send_sem=far_send_sem.at[sem_of(chunk, e)],
+                        recv_sem=far_sem.at[sem_of(chunk, e)],
                         device_id=group_at(distance),
                         device_id_type=MESH,
                     ).start()
@@ -128,32 +135,36 @@
         scatter(
             chunk,
             (
-                (k_ref, kv_bufs[chunk].at[0, side + mine], send_sem.at[0], near_sem.at[chunk]),
-                (v_ref, kv_bufs[chunk].at[1, side + mine], send_sem.at[1], near_sem.at[chunk]),
+                (k_ref, half(chunk, 0).at[side + mine], send_sem.at[0], near_sem.at[sem_of(chunk, 0)]),
+                (v_ref, half(chunk, 1).at[side + mine], send_sem.at[1], near_sem.at[sem_of(chunk, 1)]),
             ),
         )
-    for chunk in range(HEADS):
-        own = kv_bufs[chunk].at[:, pl.ds(side, GROUP)]
-        pltpu.make_async_copy(own, own, near_sem.at[chunk]).wait()
-
-        def pass_on(k, carry):
+    def pass_on(buf, which):
+        own = buf.at[:, pl.ds(side, GROUP)]
+        pltpu.make_async_copy(own, own, near_sem.at[which]).wait()
+
+        def one_place(k, carry):
             p = (mine + k) % GROUP
             for distance, first, tiles, there in far:
 
                 @pl.when((p >= first) & (p < first + tiles))
                 def _():
                     pltpu.make_async_remote_copy(
-                        src_ref=kv_bufs[chunk].at[:, side + p],
-                        dst_ref=kv_bufs[chunk].at[:, there - first + p],
-                        send_sem=far_send_sem.at[chunk],
-                        recv_sem=far_sem.at[chunk],
+                        src_ref=buf.at[:, side + p],
+                        dst_ref=buf.at[:, there - first + p],
+                        send_sem=far_send_sem.at[which],
+                        recv_sem=far_sem.at[which],
                         device_id=group_at(distance),
                         device_id_type=MESH,
                     ).start()
 
             return carry
 
-        lax.fori_loop(1, GROUP, pass_on, 0)
+        lax.fori_loop(1, GROUP, one_place, 0)
+
+    for chunk in range(HEADS):
+        for e, buf in enumerate(kv_bufs[chunk]):
+            pass_on(buf, sem_of(chunk, e))
         scatter(chunk, ((q_ref, q_buf.at[chunk, mine], send_sem.at[2], q_sem.at[chunk]),))
 
     if members > 1:
@@ -167,27 +178,41 @@
     ntiles = order_ref.shape[0]
     scale = DH ** (-0.5)
 
+    def window_place(i, c):
+        u = meta_s[i // tps, i % tps, c]
+        index = (u // tps - group * members + REACH + blk_size) % blk_size * tps + u % tps
+        return jnp.minimum(index, 2 * side + GROUP - 1)
+
+    def arrive(chunk, e):
+        buf = kv_bufs[chunk][e]
+        arrived = buf.at[:, pl.ds(0, 2 * side)]
+        pltpu.make_async_copy(arrived, arrived, far_sem.at[sem_of(chunk, e)]).wait()
+
     def attend(chunk):
-        kv = kv_bufs[chunk]
+        bufs = kv_bufs[chunk]
+
+        def key_tile(index):
+            return bufs[0][0, index]
+
+        def value_tile(index):
+            return bufs[0][1, index] if len(bufs) == 1 else bufs[1][0, index]
+
         slope = (1 << (GROUP - 1 - mine)).astype(jnp.float32) * (
             8.0 * 2.0 ** (-8.0 * chunk / H) / 2 ** (GROUP - 1) / ntiles
         )
 
-        def one_tile(i):
+        def weigh(i):
             q = q_buf[chunk, i]
-            member, row = i // tps, i % tps
-            count = meta_s[member, row, SLOTS]
+            count = meta_s[i // tps, i % tps, SLOTS]
             here = order_ref[group * GROUP + i]
-            places, biases = [], []
+            biases = []
             for c in range(SLOTS):
-                u = meta_s[member, row, c]
-                index = (u // tps - group * members + REACH + blk_size) % blk_size * tps + u % tps
-                places.append(jnp.minimum(index, kv.shape[1] - 1))
+                u = meta_s[i // tps, i % tps, c]
                 distance = jnp.abs(here - order_ref[u]).astype(jnp.float32)
                 biases.append(jnp.where(c < count, slope * distance, 1e30))
             scores = []
             for c in range(0, SLOTS, 2):
-                pair = jnp.concatenate([kv[0, places[c]], kv[0, places[c + 1]]], axis=0)
+                pair = jnp.concatenate([key_tile(window_place(i, c + e)) for e in (0, 1)], axis=0)
                 dots = lax.dot_general(
                     q, pair, (((1,), (1,)), ((), ())), preferred_element_type=jnp.float32
                 )
@@ -195,14 +220,19 @@
                     scores.append(dots[:, e * TILE : (e + 1) * TILE] * scale - biases[c + e])
             top = functools.reduce(jnp.maximum, scores)
             top = jnp.max(top, axis=1, keepdims=True)
+            return [
+                jnp.concatenate(
+                    [jnp.exp(scores[c + e] - top).astype(jnp.bfloat16) for e in (0, 1)], axis=1
+                )
+                for c in range(0, SLOTS, 2)
+            ]
+
+        def mix(i, weights):
             mixed = jnp.zeros((TILE, 2 * DH), jnp.float32)
             for c in range(0, SLOTS, 2):
-                weights = jnp.concatenate(
-                    [jnp.exp(scores[c + e] - top).astype(jnp.bfloat16) for e in (0, 1)], axis=1
-                )
-                pair = jnp.concatenate([kv[1, places[c]], kv[1, places[c + 1]]], axis=0)
+                pair = jnp.concatenate([value_tile(window_place(i, c + e)) for e in (0, 1)], axis=0)
                 mixed += jnp.dot(
-                    weights,
+                    weights[c // 2],
                     jnp.concatenate([pair, ones], axis=1),
                     preferred_element_type=jnp.float32,
                 )
@@ -226,20 +256,43 @@
                     device_id_type=MESH,
                 ).start()
 
-        def two_tiles(k, carry):
-            pair = [(mine + 1 + 2 * k + e) % GROUP for e in (0, 1)]
-            results = [one_tile(i) for i in pair]
+        def pair_at(k):
+            return [(mine + 1 + 2 * k + e) % GROUP for e in (0, 1)]
+
+        def finish(pair, results):
             for i, result in zip(pair, results):
                 o_buf[chunk, i] = result
             for i in pair:
                 send(i)
+
+        if len(bufs) == 1:
+
+            def two_tiles(k, carry):
+                pair = pair_at(k)
+                finish(pair, [mix(i, weigh(i)) for i in pair])
+                return carry
+
+            lax.fori_loop(0, GROUP // 2, two_tiles, 0)
+            return
+
+        def two_weights(k, carry):
+            pair = pair_at(k)
+            for i, weights in zip(pair, [weigh(i) for i in pair]):
+                for part in range(SLOTS // 2):
+                    w_buf[i, part] = weights[part]
             return carry
 
-        lax.fori_loop(0, GROUP // 2, two_tiles, 0)
+        def two_mixes(k, carry):
+            pair = pair_at(k)
+            finish(pair, [mix(i, [w_buf[i, part] for part in range(SLOTS // 2)]) for i in pair])
+            return carry
+
+        lax.fori_loop(0, GROUP // 2, two_weights, 0)
+        arrive(chunk, 1)
+        lax.fori_loop(0, GROUP // 2, two_mixes, 0)
 
     for chunk in range(HEADS):
-        arrived = kv_bufs[chunk].at[:, pl.ds(0, 2 * side)]
-        pltpu.make_async_copy(arrived, arrived, far_sem.at[chunk]).wait()
+        arrive(chunk, 0)
         pltpu.make_async_copy(q_buf.at[chunk], q_buf.at[chunk], q_sem.at[chunk]).wait()
         attend(chunk)
 
@@ -251,8 +304,9 @@
         part = meta_v.at[pl.ds(0, members - 1)]
         pltpu.make_async_copy(part, part, meta_sem.at[1]).wait()
     for chunk in range(HEADS):
-        arrived = kv_bufs[chunk].at[:, pl.ds(0, 2 * side)]
-        pltpu.make_async_copy(arrived, arrived, far_send_sem.at[chunk]).wait()
+        for e, buf in enumerate(kv_bufs[chunk]):
+            passed = buf.at[:, pl.ds(0, 2 * side)]
+            pltpu.make_async_copy(passed, passed, far_send_sem.at[sem_of(chunk, e)]).wait()
     part = out_ref.at[:, pl.ds(0, sent)]
     pltpu.make_async_copy(part, part, out_send_sem).wait()
     pltpu.make_async_copy(out_ref, out_ref, out_sem).wait()
@@ -271,17 +325,19 @@
         out_shape=jax.ShapeDtypeStruct(queries.shape, jnp.bfloat16),
         in_specs=[hbm, hbm, hbm, smem, smem, smem],
         out_specs=hbm,
-        scratch_shapes=[pltpu.VMEM((2, window, TILE, DH), jnp.bfloat16) for _ in range(HEADS)]
+        scratch_shapes=[pltpu.VMEM((2, window, TILE, DH), jnp.bfloat16) for _ in range(HEADS - 1)]
+        + [pltpu.VMEM((1, window, TILE, DH), jnp.bfloat16) for _ in range(2)]
         + [
             pltpu.VMEM((HEADS, GROUP, TILE, DH), jnp.bfloat16),
             pltpu.VMEM((HEADS, GROUP, TILE, DH), jnp.bfloat16),
+            pltpu.VMEM((GROUP, SLOTS // 2, TILE, 2 * TILE), jnp.bfloat16),
             pltpu.VMEM((members, META_ROWS, 128), jnp.int32),
             pltpu.SMEM((members, META_ROWS, 128), jnp.int32),
             dma((3,)),
+            dma((HEADS + 1,)),
             dma((HEADS,)),
-            dma((HEADS,)),
-            dma((HEADS,)),
-            dma((HEADS,)),
+            dma((HEADS + 1,)),
+            dma((HEADS + 1,)),
             dma,
             dma,
             dma((3,)),

time: 119 us -> 118 us (level)
  no operation moved by 1% of the time
where the time goes in v3:
time: 118 us
  Pallas kernels  115 us (97%)
  local copies, waits for them, and re-layouts  2.69 us (2%)
    pallas_call x1, Pallas kernels, body(): pl.pallas_call(functools.partial(kernel, blk_size, head_size), out_shape=...  115 us
    unnamed x1, local copies, waits for them, and re-layouts  2.69 us

profile of v3, /device:TPU:0, one launch (start us, length us, event | category | flops | bytes accessed | tf_op | source)
XLA Modules:
  0.0 118.1 jit_solution(2370809910963580098)
XLA Ops:
  0.0 115.4 %shard_map.64 = bf16[128,6144]{1,0:T(8,128)(2,1)} custom-call(bf16[128,6144]{1,0:T(8,128)(2,1)} %q_ref.1, bf16[128,6144]{1,0:T(8,128)(2,1)} %k_ref.1, bf16[128,6144]{1,0:T(8,128)(2,1)} %v_ref.1, s32[2,8]{1,0:T(2,128)} %lists_ref.1, s32[2]{0:T(128)} %counts_ref.1, s32[32]{0:T(128)} %order_ref.1), custom_call_target="tpu_custom_call" | custom-call | flops 3221225472 | bytes 6291456 | tf_op jit(solution)/shard_map/pallas_call | solution.py:323
  115.4 2.7 %copy.8 = bf16[128,6144]{1,0:T(8,128)(2,1)} copy(bf16[128,6144]{1,0:T(8,128)(2,1)} %shard_map.64) | data formatting | bytes 3145728
